TPU v7x, 1024 devices: a whole 4x4x32 slice. The times are simulated.
1024 devices in a mesh: sec: 64 (over z, core), op: 16 (over x, y).
Axes of the slice: x: 4, y: 4, z: 32, core: 2. Of those that a mesh axis runs over, the one named last changes fastest.
Arguments:
- psi: bfloat16 [3, 512, 8, 4096], P(None, 'sec'), may hold values from -23 to 23
- left_ops: bfloat16 [64, 512, 64, 64], P('op', 'sec'), may hold values from -4 to 4
- right_ops: bfloat16 [64, 512, 64, 64], P('op', 'sec'), may hold values from -4 to 4
- dest_dev: int32 [512, 8], replicated, may hold values from 0 to 63, as said below
- right_sub: int32 [512, 8], replicated, may hold values from 0 to 7
Outputs:
- sigma: bfloat16 [3, 512, 8, 4096], P(None, 'sec', None, 'op')
- subspace: float32 [3, 3], replicated
Inputs may be any that keep to these rules, and one draw needn't show every extreme that they name: `dest_dev`: the 8 entries of a row differ. Rows come in runs of 8, one run for each index of sec; within one run no value appears more than 1 times, and some value appears exactly 1 times in every run.
All inputs are finite; a program needn't handle non-finite values.
Results may differ from a plain program's by a relative error of at most 0.017.
Values may be sent and summed in bfloat16 or wider, within the bound.
A program may use at most 64 MiB of HBM per device.

v0:
```python
import jax
import jax.numpy as jnp
from jax import lax
from jax.sharding import PartitionSpec as P


def body(psi, left_ops, right_ops, dest_dev, right_sub):
    vectors, sec_local, pairs, cells = psi.shape
    terms_here = left_ops.shape[0]
    width = left_ops.shape[-1]
    devices = lax.axis_size("sec")
    groups = lax.axis_size("op")
    myself = lax.axis_index("sec")
    count = sec_local * pairs
    capacity = (count + devices - 1) // devices
    all_dest = dest_dev.reshape(devices, count)
    all_sub = right_sub.reshape(devices, count)
    my_dest = lax.dynamic_index_in_dim(all_dest, myself, 0, keepdims=False)
    blocks = psi.reshape(vectors, count, width, width)
    positions = jnp.arange(count, dtype=jnp.int32)
    earlier = (my_dest[None, :] == my_dest[:, None]) & (positions[None, :] < positions[:, None])
    place = my_dest * capacity + jnp.sum(earlier.astype(jnp.int32), axis=1)
    arriving = all_dest == myself
    ranks = jnp.cumsum(arriving.astype(jnp.int32), axis=1) - 1
    slot_index = jnp.arange(capacity, dtype=jnp.int32)[None, :, None]
    matched = arriving[:, None, :] & (ranks[:, None, :] == slot_index)
    slot_sub = jnp.sum(jnp.where(matched, all_sub[:, None, :], 0), axis=2).reshape(
        devices * capacity
    )
    right_flat = right_ops.reshape(terms_here, sec_local, cells)
    outgoing = jnp.take(right_flat, slot_sub, axis=1)
    arrived = lax.all_to_all(outgoing, "sec", split_axis=1, concat_axis=1, tiled=True)
    items = arrived.shape[0]
    chosen = arrived[:, place, :].reshape(items, count, width, width)
    contracted = jnp.einsum("vqab,tqcb->tvqac", blocks, chosen, preferred_element_type=jnp.float32)
    inner = contracted.astype(jnp.bfloat16).reshape(items, vectors, count, cells)
    inner_tiles = inner.reshape(terms_here, vectors, sec_local, pairs, width, width)
    partial_sigma = jnp.einsum(
        "tsab,tvspbc->vspac", left_ops, inner_tiles, preferred_element_type=jnp.float32
    )
    partial_sigma = partial_sigma.reshape(vectors, sec_local, pairs, cells)
    share = cells // groups
    summed = lax.psum(partial_sigma.astype(jnp.bfloat16), "op").astype(jnp.float32)
    sigma_share = lax.dynamic_slice_in_dim(summed, lax.axis_index("op") * share, share, 3)
    entries = sec_local * devices * pairs * cells
    psi_share = lax.dynamic_slice_in_dim(psi, lax.axis_index("op") * share, share, 3)
    local_terms = jnp.einsum(
        "vapx,wapx->vw", psi_share.astype(jnp.float32), sigma_share, precision=lax.Precision.HIGHEST
    )
    subspace = lax.psum(local_terms, ("sec", "op")) / entries
    return (sigma_share.astype(jnp.bfloat16), subspace)


def solution(mesh):
    return jax.shard_map(
        body,
        mesh=mesh,
        in_specs=(
            P(None, "sec", None, None),
            P("op", "sec", None, None),
            P("op", "sec", None, None),
            P(),
            P(),
        ),
        out_specs=(P(None, "sec", None, "op"), P()),
        check_vma=False,
    )
```

profile of v0, /device:TPU:1, one launch (start us, length us, event | category | flops | bytes accessed | tf_op | source)
XLA Modules:
  0.0 599.1 jit_solution(17767620482301456976)
XLA Ops:
  7.2 0.0 copy-start
  7.2 0.8 broadcast_compare_fusion
  8.0 0.2 copy.26
  8.1 0.2 eq.50
  8.3 0.8 copy.27
  9.2 0.1 broadcast_in_dim_reshape.3
  9.3 0.2 reduce_window_sum.11
  9.5 0.1 select_reduce_fusion
  9.7 1.5 reshape.133
  11.2 0.2 copy.42
  11.4 2.4 gather_fusion
  13.8 2.4 select_bitcast_fusion
  16.1 0.0 copy-start.2
  16.1 0.0 copy-start.1
  16.1 30.7 %all-to-all-start = ((bf16[4,64,4096]{2,0,1:T(4,128)(2,1)}), bf16[4,64,4096]{2,0,1:T(4,128)(2,1)}, u32[]{:S(2)}, u32[]{:S(2)}) async-start(bf16[4,64,4096]{2,0,1:T(4,128)(2,1)} %select_bitcast_fusion), calls=%async_computation | async-start | bytes 4194304 | tf_op jit(solution)/shard_map/all_to_all | solution.py:32
  46.9 0.2 all-reduce.2.cloned.1.call-start
  47.1 0.0 copy-done.2
  47.1 0.1 copy.29
  47.2 0.1 reshape.109
  47.4 0.0 copy-done.1
  47.4 4.4 reshape.111
  51.8 0.2 convert_reduce_fusion
  52.0 192.5 %all-to-all-done = bf16[4,64,4096]{2,0,1:T(4,128)(2,1)} async-done(((bf16[4,64,4096]{2,0,1:T(4,128)(2,1)}), bf16[4,64,4096]{2,0,1:T(4,128)(2,1)}, u32[]{:S(2)}, u32[]{:S(2)}) %all-to-all-start) | async-done | bytes 2097184 | tf_op jit(solution)/shard_map/all_to_all | solution.py:32
  244.5 4.0 gather_fusion.1
  248.5 4.6 reshape.128
  253.0 10.7 %convolution_convert_fusion = bf16[64,4,64,3,64]{4,2,3,1,0:T(8,128)(2,1)} fusion(bf16[4,64,64,64,1]{3,2,0,1,4:T(8,128)(2,1)} %reshape.128, bf16[3,64,64,64]{3,2,1,0:T(8,128)(2,1)} %reshape.111), kind=kOutput, calls=%fused_computation.4 | convolution fusion | flops 405798912 | bytes 9961472 | tf_op jit(solution)/shard_map/vqab,tqcb->tvqac/dot_general | solution.py:35
  263.7 0.0 copy-done
  263.7 9.7 %fusion.3 = bf16[3,8,8,64,64]{3,4,2,0,1:T(8,128)(2,1)} fusion(bf16[4,3,8,8,64,64]{4,5,1,0,3,2:T(8,128)(2,1)} %bitcast.52, bf16[4,8,64,64]{3,2,1,0:T(8,128)(2,1)S(1)} %copy-done), kind=kOutput, calls=%fused_computation.7 | convolution fusion | flops 403439616 | bytes 8126464 | tf_op jit(solution)/shard_map/tsab,tvspbc->vspac/dot_general | solution.py:38
  273.4 4.6 copy.47
  278.0 6.9 %reshape.135 = bf16[3,8,8,4096]{3,0,2,1:T(4,128)(2,1)} reshape(bf16[3,8,8,64,64]{4,3,0,2,1:T(8,128)(2,1)} %copy.47) | data formatting | bytes 3145728 | tf_op jit(solution)/shard_map/convert_element_type | solution.py:43
  284.9 0.0 all-reduce.2.cloned.1.call-update
  284.9 0.9 constant_dynamic-slice_fusion
  285.8 144.2 %all-reduce.2.cloned.1.call-done = bf16[3,8,8,4096]{3,0,2,1:T(4,128)(2,1)} async-done(((bf16[3,8,8,4096]{3,0,2,1:T(4,128)(2,1)}), bf16[3,8,8,4096]{3,0,2,1:T(4,128)(2,1)}) %all-reduce.2.cloned.1.call-update) | async-done | bytes 1572880 | tf_op jit(solution)/shard_map/psum | solution.py:43
  430.0 1.2 convolution_bitcast_fusion
  431.2 158.8 %psum.15 = f32[3,3]{1,0:T(4,128)S(1)} all-reduce(f32[3,3]{1,0:T(4,128)S(1)} %convolution_bitcast_fusion), channel_id=1, replica_groups=mesh['sec'=64,'op'=16] {'sec','op'}, use_global_device_ids=true, to_apply=%region_4.5 | all-reduce | flops 9 | bytes 72 | tf_op jit(solution)/shard_map/psum | solution.py:50
  590.0 0.6 broadcast_multiply_fusion
  590.6 1.0 convert_convert_fusion
  591.6 0.7 copy.36
  (7 shorter events, 0.0 us)
Async XLA Ops:
  7.2 256.6 %copy-start = (bf16[4,8,64,64]{3,2,1,0:T(8,128)(2,1)S(1)}, bf16[4,8,64,64]{3,2,1,0:T(8,128)(2,1)}, u32[]{:S(2)}) copy-start(bf16[4,8,64,64]{3,2,1,0:T(8,128)(2,1)} %param.6) | copy-start | bytes 786436
  16.1 31.0 %copy-start.2 = (s32[512,8]{0,1:T(8,128)S(1)}, s32[512,8]{0,1:T(8,128)}, u32[]{:S(2)}) copy-start(s32[512,8]{0,1:T(8,128)} %param.8) | copy-start | bytes 49156
  16.1 31.2 %copy-start.1 = (bf16[3,8,8,4096]{3,2,1,0:T(8,128)(2,1)S(1)}, bf16[3,8,8,4096]{3,2,1,0:T(8,128)(2,1)}, u32[]{:S(2)}) copy-start(bf16[3,8,8,4096]{3,2,1,0:T(8,128)(2,1)} %param.5) | copy-start | bytes 4718596
  16.1 228.4 %all-to-all-start = ((bf16[4,64,4096]{2,0,1:T(4,128)(2,1)}), bf16[4,64,4096]{2,0,1:T(4,128)(2,1)}, u32[]{:S(2)}, u32[]{:S(2)}) async-start(bf16[4,64,4096]{2,0,1:T(4,128)(2,1)} %select_bitcast_fusion), calls=%async_computation | async-start | bytes 4194304 | tf_op jit(solution)/shard_map/all_to_all | solution.py:32
  46.9 383.1 %all-reduce.2.cloned.1.call-start = ((), (), s32[]{:S(2)}) async-start(), calls=%async_computation.1 | async-start | bytes 4194304 | tf_op jit(solution)/shard_map/psum | solution.py:43
Sparse Core Ops, SparseCore 0:
  285.0 144.8 all-reduce.1
where the time goes:
time: 600 us; the launch traced here: 599 us
  waiting for transfers between devices  337 us (56%)
  blocking collectives  159 us (26%)
  local copies, waits for them, and re-layouts  31.6 us (5%)
  starting transfers between devices  30.9 us (5%)
  matrix products  21.6 us (4%)
  between operations  14.2 us (2%)
    all_to_all x1, waiting for transfers between devices, body(): lax.all_to_all(outgoing, 'sec', split_axis=1, concat_axis=1, tiled=True)  193 us
    psum x1, blocking collectives, body(): subspace = lax.psum(local_terms, ('sec', 'op')) / entries  159 us
    psum x1, waiting for transfers between devices, body(): lax.psum(partial_sigma.astype(jnp.bfloat16), 'op').astype(jnp.float32)  144 us
    all_to_all x1, starting transfers between devices, body(): lax.all_to_all(outgoing, 'sec', split_axis=1, concat_axis=1, tiled=True)  30.7 us
  transfers between devices with their start and end apart: 2, of which 2 were waited for; matrix products, arithmetic and copies ran while one was open for 1% of the time, Pallas kernels for 0%

commit v1 on v0

v1 whole, which is shorter than its diff:
```python
import functools

import jax
import jax.numpy as jnp
from jax import lax
from jax.experimental import pallas as pl
from jax.experimental.pallas import tpu as pltpu
from jax.sharding import PartitionSpec as P

MESH = pl.DeviceIdType.MESH
CHUNKS = 2
F32 = jnp.float32
BF16 = jnp.bfloat16


def kernel(
    chips, groups, scale,
    tab_ref, idx_ref, psi_ref, left_ref, right_ref,
    sig_ref, sub_ref,
    ring, blk, pass_on, wide, lefts, stage, outbox, inbox, total, acc,
    dots, dots_op, dots_core, dots_chip, one, two, three, shelf,
    ring_send, ring_recv, pair_send, pair_recv, op_send, op_recv, dot_send, dot_recv,
):
    half = chips // 2
    vectors, secs, pairs, cells = psi_ref.shape
    batches = chips // 4
    per = secs // CHUNKS
    me = lax.axis_index("sec")
    core = lax.rem(me, 2)
    z = lax.div(me, 2)
    op = lax.axis_index("op")
    mate = z * 2 + 1 - core

    def chip(step):
        return lax.rem(z + step + chips, chips) * 2 + core

    def op_peer(step):
        return lax.rem(op + step, groups)

    barrier = pltpu.get_barrier_semaphore()

    def greet_chip(step, carry):
        pl.semaphore_signal(barrier, inc=1, device_id={"sec": chip(step)}, device_id_type=MESH)
        return carry

    def greet_op(step, carry):
        pl.semaphore_signal(barrier, inc=1, device_id={"op": op_peer(step)}, device_id_type=MESH)
        return carry

    lax.fori_loop(1, chips, greet_chip, 0)
    if groups > 1:
        lax.fori_loop(1, groups, greet_op, 0)
    pl.semaphore_signal(barrier, inc=1, device_id={"sec": mate}, device_id_type=MESH)

    def pack_right(s, carry):
        for high in range(2):
            ring[0, s, high * 64:(high + 1) * 64, :] = jnp.concatenate(
                [right_ref[2 * high, s], right_ref[2 * high + 1, s]], axis=1
            )
        return carry

    lax.fori_loop(0, secs, pack_right, 0)
    pl.semaphore_wait(barrier, chips + groups - 1)

    def ring_copy(way, hop, q):
        if way == 0:
            src, dst, target = hop - 1, hop, chip(1)
        else:
            src, dst, target = lax.rem(chips + 1 - hop, chips), chips - hop, chip(-1)
        return pltpu.make_async_remote_copy(
            src_ref=ring.at[src, pl.ds(q * per, per)],
            dst_ref=ring.at[dst, pl.ds(q * per, per)],
            send_sem=ring_send.at[way, hop, q],
            recv_sem=ring_recv.at[way, hop, q],
            device_id={"sec": target},
            device_id_type=MESH,
        )

    def last_way(q):
        return 0 if q < CHUNKS // 2 else 1

    for q in range(CHUNKS):
        ring_copy(0, 1, q).start()
        ring_copy(1, 1, q).start()

    def pair_copy(slot):
        return pltpu.make_async_remote_copy(
            src_ref=pass_on.at[slot],
            dst_ref=blk.at[chips + slot],
            send_sem=pair_send.at[slot],
            recv_sem=pair_recv.at[slot],
            device_id={"sec": mate},
            device_id_type=MESH,
        )

    def choose(slot):
        for s in range(secs):
            shelf[s] = ring[slot, s]
        pass_on[slot] = shelf[tab_ref[2, chips + slot]]
        pair_copy(slot).start()
        blk[slot] = shelf[tab_ref[2, slot]]

    choose(0)

    low = lax.broadcasted_iota(jnp.int32, (pairs, 128), 1) < 64

    def widen(step, carry):
        v = lax.div(step, secs)
        l = lax.rem(step, secs)
        for t in range(cells // 128):
            x = psi_ref[v, l, :, t * 128:(t + 1) * 128].astype(F32)
            r = pltpu.roll(x, 64, 1)
            wide[v, l, pl.ds(2 * t, pairs, stride=64), :] = jnp.where(low, x, r)
            wide[v, l, pl.ds(2 * t + 1, pairs, stride=64), :] = jnp.where(low, r, x)
        return carry

    lax.fori_loop(0, vectors * secs, widen, 0)

    def pack_left(l, carry):
        for high in range(2):
            lefts[l, high * 64:(high + 1) * 64, :] = jnp.concatenate(
                [left_ref[2 * high, l], left_ref[2 * high + 1, l]], axis=1
            )
        return carry

    lax.fori_loop(0, secs, pack_left, 0)
    acc[...] = jnp.zeros_like(acc)
    low64 = lax.broadcasted_iota(jnp.int32, (64, 128), 1) < 64

    def rows_of(v, l, p):
        return wide[v, l, pl.ds(p * 64, 64), :]

    def pair(slot, n):
        found = []
        tiles = []
        for w in range(2):
            l = tab_ref[0, w * chips + slot]
            p = tab_ref[1, w * chips + slot]
            mat = blk[w * chips + slot]
            ys = [rows_of(v, l, p) for v in range(vectors)]
            tiles.append(ys)
            lhs = jnp.concatenate(
                [jnp.where(low64, y, 0.0).astype(BF16) for y in ys]
                + [jnp.where(low64, 0.0, y).astype(BF16) for y in ys], axis=0
            )
            inner = lax.dot_general(
                lhs, mat, (((1,), (1,)), ((), ())), preferred_element_type=F32
            ).astype(BF16)
            rhs = jnp.concatenate(
                [
                    jnp.concatenate(
                        [inner[v * 64:(v + 1) * 64], inner[(vectors + v) * 64:(vectors + v + 1) * 64]],
                        axis=0,
                    )
                    for v in range(vectors)
                ],
                axis=1,
            )
            out = jnp.dot(lefts[l], rhs, preferred_element_type=F32)
            sums = []
            for v in range(vectors):
                top = out[0:64, v * 128:(v + 1) * 128]
                bottom = out[64:128, v * 128:(v + 1) * 128]
                if w == 0:
                    sums.append(top + pltpu.roll(bottom, 64, 1))
                else:
                    sums.append(pltpu.roll(top, 64, 1) + bottom)
            found.append(sums)
        parts = []
        for v in range(vectors):
            part = jnp.where(low64, found[0][v], found[1][v]).astype(BF16).astype(F32)
            stage[lax.rem(n, 4), v] = part
            parts.append(part)
        for v in range(vectors):
            both = jnp.where(low64, tiles[0][v], tiles[1][v])
            for w in range(vectors):
                prod = (both * parts[w]).reshape(8, 8, 128)
                acc[v * vectors + w] += jnp.sum(prod, axis=0)

    low4 = lax.broadcasted_iota(jnp.int32, (8, 8, 128), 1) < 4

    def op_copy(step, batch):
        peer = op_peer(step)
        return pltpu.make_async_remote_copy(
            src_ref=outbox.at[batch, peer],
            dst_ref=inbox.at[batch, op],
            send_sem=op_send.at[batch],
            recv_sem=op_recv.at[batch],
            device_id={"op": peer},
            device_id_type=MESH,
        )

    def finish(batch):
        for v in range(vectors):
            xs = [stage[j, v].reshape(8, 8, 128) for j in range(4)]
            ev, od = [], []
            for j in (0, 2):
                x, y = xs[j], xs[j + 1]
                ev.append(jnp.where(low4, x, pltpu.roll(y, 4, 1)))
                od.append(jnp.where(low4, pltpu.roll(x, 4, 1), y))
            even = jnp.concatenate(ev, axis=1).astype(BF16)
            odd = jnp.concatenate(od, axis=1).astype(BF16)
            for t in range(8):
                outbox[batch, 2 * t, v * 16:(v + 1) * 16, :] = even[t]
                outbox[batch, 2 * t + 1, v * 16:(v + 1) * 16, :] = odd[t]
        if groups > 1:

            def send(step, carry):
                op_copy(step, batch).start()
                return carry

            lax.fori_loop(1, groups, send, 0)
        inbox[batch, op] = outbox[batch, op]

    def gather_sum(batch):
        if groups > 1:
            pltpu.make_async_remote_copy(
                src_ref=outbox.at[batch, pl.ds(0, groups - 1)],
                dst_ref=inbox.at[batch, pl.ds(0, groups - 1)],
                send_sem=op_send.at[batch],
                recv_sem=op_recv.at[batch],
                device_id={"op": op_peer(1)},
                device_id_type=MESH,
            ).wait()
        value = inbox[batch, 0].astype(F32)
        for g in range(1, groups):
            value += inbox[batch, g].astype(F32)
        total[batch] = value.astype(BF16)

    def turn(h, carry):
        def serve(q):
            for way in range(2):
                ring_copy(way, h, q).wait_recv()
                if last_way(q) == way:
                    ring_copy(way, h + 1, q).start()
                else:

                    @pl.when(h < half - 1)
                    def _():
                        ring_copy(way, h + 1, q).start()

        for q in range(CHUNKS // 2):
            serve(q)
        pair_copy(h - 1).wait_recv()
        first = 2 * (h - 1) - 1 + lax.div(half - h, half - 1)
        pair(h - 1, first)

        @pl.when(jnp.logical_and(lax.rem(h, 2) == 1, h >= 3))
        def _():
            finish(lax.div(h - 3, 2))

        for q in range(CHUNKS // 2, CHUNKS):
            serve(q)

        @pl.when(h >= 2)
        def _():
            pair_copy(chips - (h - 1)).wait_recv()
            pair(chips - (h - 1), 2 * (h - 1))

        choose(h)
        choose(chips - h)

        @pl.when(jnp.logical_and(lax.rem(h, 2) == 1, h >= 5))
        def _():
            gather_sum(lax.div(h - 5, 2))

        return carry

    lax.fori_loop(1, half, turn, 0)

    for q in range(CHUNKS):
        ring_copy(last_way(q), half, q).wait_recv()
    choose(half)
    pair_copy(half - 1).wait_recv()
    pair(half - 1, 2 * half - 3)
    pair_copy(half + 1).wait_recv()
    pair(half + 1, 2 * half - 2)
    pair_copy(half).wait_recv()
    pair(half, 2 * half - 1)
    finish(batches - 1)

    dots[...] = jnp.zeros_like(dots)
    for i in range(vectors * vectors):
        dots[i:i + 1, :] = jnp.sum(acc[i], axis=0, keepdims=True)
    if groups > 1:

        def dot_copy(step):
            return pltpu.make_async_remote_copy(
                src_ref=dots,
                dst_ref=dots_op.at[op],
                send_sem=dot_send.at[0],
                recv_sem=dot_recv.at[0],
                device_id={"op": op_peer(step)},
                device_id_type=MESH,
            )

        def send_dots(step, carry):
            dot_copy(step).start()
            return carry

        lax.fori_loop(1, groups, send_dots, 0)
    dots_op[op] = dots[...]

    if batches > 1:
        gather_sum(batches - 2)

    if groups > 1:
        pltpu.make_async_remote_copy(
            src_ref=dots_op.at[pl.ds(0, groups - 1)],
            dst_ref=dots_op.at[pl.ds(0, groups - 1)],
            send_sem=dot_send.at[0],
            recv_sem=dot_recv.at[0],
            device_id={"op": op_peer(1)},
            device_id_type=MESH,
        ).wait()
    value = dots_op[0]
    for g in range(1, groups):
        value += dots_op[g]
    one[...] = value
    core_copy = pltpu.make_async_remote_copy(
        src_ref=one,
        dst_ref=dots_core,
        send_sem=dot_send.at[1],
        recv_sem=dot_recv.at[1],
        device_id={"sec": mate},
        device_id_type=MESH,
    )
    core_copy.start()
    gather_sum(batches - 1)
    core_copy.wait()
    two[...] = one[...] + dots_core[...]

    def send_chip(step, carry):
        pltpu.make_async_remote_copy(
            src_ref=two,
            dst_ref=dots_chip.at[z],
            send_sem=dot_send.at[2],
            recv_sem=dot_recv.at[2],
            device_id={"sec": chip(step)},
            device_id_type=MESH,
        ).start()
        return carry

    lax.fori_loop(1, chips, send_chip, 0)
    dots_chip[z] = two[...]

    code = idx_ref[...]
    second = lax.rem(code, 2) == 1
    base = lax.div(code, 2) * 4
    column = lax.broadcasted_iota(jnp.int32, (64, 128), 1)
    rows = total.shape[0] * 16
    for v in range(vectors):
        table = total[:, v * 16:(v + 1) * 16, :].reshape(rows, 128)
        got = []
        for i in range(4):
            hot = jnp.where(column[:idx_ref.shape[0], :rows] == base[:, :rows] + i, 1.0, 0.0).astype(BF16)
            got.append(jnp.dot(hot, table, preferred_element_type=F32))
        lanes = column[:idx_ref.shape[0]] < 64
        for i in range(2):
            x = jnp.where(second, pltpu.roll(got[2 * i], 64, 1), got[2 * i])
            y = jnp.where(second, got[2 * i + 1], pltpu.roll(got[2 * i + 1], 64, 1))
            sig_ref[v, :, i * 128:(i + 1) * 128] = jnp.where(lanes, x, y).astype(BF16)

    def drain(h, carry):
        for q in range(CHUNKS):
            for way in range(2):
                if last_way(q) == way:
                    ring_copy(way, h, q).wait_send()
                else:

                    @pl.when(h < half)
                    def _():
                        ring_copy(way, h, q).wait_send()

        return carry

    lax.fori_loop(1, half + 1, drain, 0)

    def drain_pairs(slot, carry):
        pair_copy(slot).wait_send()
        return carry

    lax.fori_loop(0, chips, drain_pairs, 0)

    pltpu.make_async_remote_copy(
        src_ref=dots_chip.at[pl.ds(0, chips - 1)],
        dst_ref=dots_chip.at[pl.ds(0, chips - 1)],
        send_sem=dot_send.at[2],
        recv_sem=dot_recv.at[2],
        device_id={"sec": chip(1)},
        device_id_type=MESH,
    ).wait()
    value = dots_chip[0]
    for g in range(1, chips):
        value += dots_chip[g]
    three[...] = jnp.sum(value, axis=1, keepdims=True) * scale
    for v in range(vectors):
        for w in range(vectors):
            i = v * vectors + w
            sub_ref[v:v + 1, w:w + 1] = three[i:i + 1, :]


def body(psi, left_ops, right_ops, dest_dev, right_sub):
    vectors, secs, pairs, cells = psi.shape
    terms = left_ops.shape[0]
    devices = lax.axis_size("sec")
    groups = lax.axis_size("op")
    chips = devices // 2
    count = secs * pairs
    me = lax.axis_index("sec")
    core = me % 2
    z = me // 2
    all_dest = dest_dev.reshape(devices, count)
    all_sub = right_sub.reshape(devices, count)
    my_dest = lax.dynamic_index_in_dim(all_dest, me, 0, keepdims=False)
    my_sub = lax.dynamic_index_in_dim(all_sub, me, 0, keepdims=False)
    mate = z * 2 + 1 - core
    mate_dest = lax.dynamic_index_in_dim(all_dest, mate, 0, keepdims=False)
    mate_sub = lax.dynamic_index_in_dim(all_sub, mate, 0, keepdims=False)
    slots = jnp.arange(chips, dtype=jnp.int32)
    source = ((z - slots + chips) % chips) * 2
    same = source + core
    both = jnp.concatenate([same, source + 1 - core])
    places = jnp.arange(count, dtype=jnp.int32)
    hit = both[:, None] == my_dest[None, :]
    where = jnp.sum(jnp.where(hit, places[None, :], 0), axis=1)
    mine = jnp.sum(jnp.where(hit[:chips], my_sub[None, :], 0), axis=1)
    theirs = jnp.sum(
        jnp.where(same[:, None] == mate_dest[None, :], mate_sub[None, :], 0), axis=1
    )
    tab = jnp.stack([where // pairs, where % pairs, jnp.concatenate([mine, theirs])])
    slot = (z - my_dest // 2 + chips) % chips
    half = chips // 2
    order = jnp.where(
        slot == 0, 0, jnp.where(slot == half, chips - 1, jnp.where(slot < half, 2 * slot - 1, 2 * (chips - slot)))
    )
    code = order * 2 + (my_dest % 2 != core).astype(jnp.int32)
    idx = jnp.broadcast_to(code[:, None], (count, 128))
    entries = secs * devices * pairs * cells
    batches = chips // 4
    vmem = pltpu.VMEM
    dma = pltpu.SemaphoreType.DMA
    sigma, subspace = pl.pallas_call(
        functools.partial(kernel, chips, groups, 1.0 / entries),
        out_shape=(
            jax.ShapeDtypeStruct((vectors, count, cells // 16), BF16),
            jax.ShapeDtypeStruct((vectors, vectors), F32),
        ),
        in_specs=[pl.BlockSpec(memory_space=pltpu.SMEM)]
        + [pl.BlockSpec(memory_space=pltpu.VMEM)] * 4,
        out_specs=(pl.BlockSpec(memory_space=pltpu.VMEM), pl.BlockSpec(memory_space=pltpu.VMEM)),
        scratch_shapes=[
            vmem((chips, secs, 128, 128), BF16),
            vmem((2 * chips, 128, 128), BF16),
            vmem((chips, 128, 128), BF16),
            vmem((vectors, secs, pairs * 64, 128), F32),
            vmem((secs, 128, 128), BF16),
            vmem((4, vectors, 64, 128), F32),
            vmem((batches, 16, vectors * 16, 128), BF16),
            vmem((batches, groups, vectors * 16, 128), BF16),
            vmem((batches, vectors * 16, 128), BF16),
            vmem((vectors * vectors, 8, 128), F32),
            vmem((16, 128), F32),
            vmem((groups, 16, 128), F32),
            vmem((16, 128), F32),
            vmem((chips, 16, 128), F32),
            vmem((16, 128), F32),
            vmem((16, 128), F32),
            vmem((16, 1), F32),
            vmem((secs, 128, 128), BF16),
            dma((2, half + 1, CHUNKS)),
            dma((2, half + 1, CHUNKS)),
            dma((chips,)),
            dma((chips,)),
            dma((batches,)),
            dma((batches,)),
            dma((3,)),
            dma((3,)),
        ],
        compiler_params=pltpu.CompilerParams(
            collective_id=0, has_side_effects=True, vmem_limit_bytes=48 * 1024 * 1024
        ),
        cost_estimate=pl.CostEstimate(
            flops=4 * terms * vectors * count * 64 ** 3, bytes_accessed=8 << 20, transcendentals=0
        ),
    )(tab, idx, psi, left_ops, right_ops)
    return sigma.reshape(vectors, secs, pairs, cells // 16), subspace


def solution(mesh):
    return jax.shard_map(
        body,
        mesh=mesh,
        in_specs=(
            P(None, "sec", None, None),
            P("op", "sec", None, None),
            P("op", "sec", None, None),
            P(),
            P(),
        ),
        out_specs=(P(None, "sec", None, "op"), P()),
        check_vma=False,
    )
```

time: 600 us -> 170 us (0.28)
  waiting for transfers between devices: 337 us -> 0 us
  Pallas kernels: 0 us -> 162 us
  blocking collectives: 159 us -> 0 us
  starting transfers between devices: 30.9 us -> 0 us
  local copies, waits for them, and re-layouts: 31.6 us -> 6.74 us
  matrix products: 21.6 us -> 0 us
  between operations: 14.2 us -> 0.74 us
    all_to_all x1 -> x0, waiting for transfers between devices: 193 us -> none  [body(): lax.all_to_all(outgoing, 'sec', split_axis=1, concat_axis=1, tiled=True)]
    pallas_call x0 -> x1, Pallas kernels: none -> 162 us  [body(): pl.pallas_call(functools.partial(kernel, chips, groups, 1.0 / entries), o...]
    psum x1 -> x0, blocking collectives: 159 us -> none  [body(): subspace = lax.psum(local_terms, ('sec', 'op')) / entries]
    psum x1 -> x0, waiting for transfers between devices: 144 us -> none  [body(): lax.psum(partial_sigma.astype(jnp.bfloat16), 'op').astype(jnp.float32)]
    all_to_all x1 -> x0, starting transfers between devices: 30.7 us -> none  [body(): lax.all_to_all(outgoing, 'sec', split_axis=1, concat_axis=1, tiled=True)]
    dot_general x3 -> x0, matrix products: 21.6 us -> none  [the longest x1 10.7 us: body(): jnp.einsum('vqab,tqcb->tvqac', blocks, chosen, preferred_element_type=jnp...]
    convert_element_type x2 -> x0, local copies, waits for them, and re-layouts: 11.5 us -> none  [body(): partial_sigma.astype(jnp.bfloat16)]
    reshape x4 -> x1, local copies, waits for them, and re-layouts: 10.6 us -> 0.13 us  [body(): all_sub = right_sub.reshape(devices, count)]
  transfers between devices with their start and end apart: 2 -> 0, of which waited for: 2 -> 0; matrix products, arithmetic and copies ran while one was open for 1% -> 0% of each run, Pallas kernels for 0% -> 0%
where the time goes in v1:
time: 170 us
  Pallas kernels  162 us (95%)
  local copies, waits for them, and re-layouts  6.74 us (4%)
    pallas_call x1, Pallas kernels, body(): pl.pallas_call(functools.partial(kernel, chips, groups, 1.0 / entries), o...  162 us
    unnamed x10, local copies, waits for them, and re-layouts  6.39 us

profile of v1, /device:TPU:1, one launch (start us, length us, event | category | flops | bytes accessed | tf_op | source)
XLA Modules:
  0.0 170.1 jit_solution(11582510860525676390)
XLA Ops:
  0.6 0.8 copy.10
  1.5 0.1 reshape.180
  1.6 0.8 copy.9
  2.5 0.1 reshape.179
  2.7 0.2 select_reduce_fusion.1
  2.9 0.1 fusion.6
  2.9 0.1 broadcast_compare_fusion
  3.0 0.1 select_reduce_fusion.2
  3.1 0.1 add_bitcast_fusion
  3.2 0.2 select_reduce_fusion
  3.4 0.1 broadcast_in_dim.57.idx_ref
  3.5 0.0 copy-start
  3.5 1.4 copy-done
  4.9 0.0 copy-start.1
  4.9 1.0 copy-done.1
  6.0 0.0 copy-start.2
  6.0 1.0 copy-done.2
  7.0 161.9 %shard_map.68 = (bf16[3,64,256]{2,1,0:T(8,128)(2,1)S(1)}, f32[3,3]{1,0:T(4,128)S(1)}) custom-call(s32[3,64]{1,0:T(4,128)S(1)} %pad_add_fusion.tab_ref, s32[64,128]{1,0:T(8,128)S(1)} %broadcast_in_dim.57.idx_ref, bf16[3,8,8,4096]{3,2,1,0:T(8,128)(2,1)S(1)} %copy-done, bf16[4,8,64,64]{3,2,1,0:T(8,128)(2,1)S(1)} %copy-done.1, bf16[4,8,64,64]{3,2,1,0:T(8,128)(2,1)S(1)} %copy-done.2), custom_call_target="tpu_custom_call" | custom-call | flops 805306368 | bytes 8388608 | tf_op jit(solution)/shard_map/pallas_call | solution.py:443
  168.9 0.6 copy.13
  169.5 0.6 copy.14
  (5 shorter events, 0.1 us)
Async XLA Ops:
  3.5 1.4 copy-start
  4.9 1.0 copy-start.1
  6.0 1.0 copy-start.2

commit v2 on v1

--- a/solution.py
+++ b/solution.py
@@ -9,19 +9,21 @@
 
 MESH = pl.DeviceIdType.MESH
 CHUNKS = 2
+FAR = 4
 F32 = jnp.float32
 BF16 = jnp.bfloat16
 
 
 def kernel(
     chips, groups, scale,
-    tab_ref, idx_ref, psi_ref, left_ref, right_ref,
+    psi_hbm, left_hbm, right_hbm, dest_hbm, choice_hbm,
     sig_ref, sub_ref,
-    ring, blk, pass_on, wide, lefts, stage, outbox, inbox, total, acc,
-    dots, dots_op, dots_core, dots_chip, one, two, three, shelf,
-    ring_send, ring_recv, pair_send, pair_recv, op_send, op_recv, dot_send, dot_recv,
+    psi_ref, left_ref, right_ref, dest_ref, choice_ref, lists, tab_ref, code_ref, ring, far, blk, pass_on, wide, lefts, stage, outbox, inbox, total, acc,
+    dots, dots_op, dots_core, dots_chip, one, two, shelf,
+    load_sem, ring_send, ring_recv, far_send, far_recv, pair_send, pair_recv, op_send, op_recv, dot_send, dot_recv,
 ):
     half = chips // 2
+    near = half - FAR
     vectors, secs, pairs, cells = psi_ref.shape
     batches = chips // 4
     per = secs // CHUNKS
@@ -37,20 +39,36 @@
     def op_peer(step):
         return lax.rem(op + step, groups)
 
+    loads = [
+        pltpu.make_async_copy(src, dst, load_sem.at[i])
+        for i, (src, dst) in enumerate(
+            (
+                (right_hbm, right_ref),
+                (dest_hbm, dest_ref),
+                (choice_hbm, choice_ref),
+                (psi_hbm, psi_ref),
+                (left_hbm, left_ref),
+            )
+        )
+    ]
+    for load in loads:
+        load.start()
+
     barrier = pltpu.get_barrier_semaphore()
 
-    def greet_chip(step, carry):
-        pl.semaphore_signal(barrier, inc=1, device_id={"sec": chip(step)}, device_id_type=MESH)
-        return carry
+    def greet(where):
+        pl.semaphore_signal(barrier, inc=1, device_id=where, device_id_type=MESH)
 
     def greet_op(step, carry):
-        pl.semaphore_signal(barrier, inc=1, device_id={"op": op_peer(step)}, device_id_type=MESH)
-        return carry
-
-    lax.fori_loop(1, chips, greet_chip, 0)
+        greet({"op": op_peer(step)})
+        return carry
+
+    greet({"sec": chip(1)})
+    greet({"sec": chip(-1)})
+    greet({"sec": mate})
     if groups > 1:
         lax.fori_loop(1, groups, greet_op, 0)
-    pl.semaphore_signal(barrier, inc=1, device_id={"sec": mate}, device_id_type=MESH)
+    greetings = 3 + (groups - 1)
 
     def pack_right(s, carry):
         for high in range(2):
@@ -59,8 +77,79 @@
             )
         return carry
 
+    loads[0].wait()
     lax.fori_loop(0, secs, pack_right, 0)
-    pl.semaphore_wait(barrier, chips + groups - 1)
+    rows = 4 * chips
+    loads[1].wait()
+    loads[2].wait()
+    total_secs = dest_ref.shape[1]
+    width = min(128, total_secs)
+    if width == 128:
+        start = pl.multiple_of(lax.div(me * secs, width) * width, width)
+    else:
+        start = 0
+    near_dest = dest_ref[:, pl.ds(start, width)]
+    near_choice = choice_ref[:, pl.ds(start, width)]
+
+    def step_of(shape):
+        return lax.shift_right_logical(lax.broadcasted_iota(jnp.int32, shape, 0), 2)
+
+    def source_of(n):
+        odd = lax.rem(n, 2)
+        half_n = lax.shift_right_logical(n + odd, 1)
+        slot = jnp.where(odd == 1, half_n, chips - half_n)
+        return lax.rem(z - slot + 2 * chips, chips) * 2
+
+    source = source_of(step_of((rows, width)))
+    sector = lax.broadcasted_iota(jnp.int32, (1, width), 1) + start
+    holder = lax.div(sector, secs)
+    inside = lax.rem(sector, secs)
+    count = secs * pairs
+    block_l = lax.div(lax.broadcasted_iota(jnp.int32, (count, width), 0), pairs)
+    block_p = lax.rem(lax.broadcasted_iota(jnp.int32, (count, width), 0), pairs)
+    found = [jnp.zeros((rows, width), jnp.int32) for _ in range(4)]
+    target = jnp.zeros((count, width), jnp.int32)
+    for p in range(pairs):
+        here = jnp.where(holder == me, near_dest[p:p + 1], -1)
+        there = jnp.where(holder == mate, near_dest[p:p + 1], -1)
+        pick = near_choice[p:p + 1]
+        hits = (here == source + core, here == source + 1 - core, there == source + core)
+        place = inside * pairs + p
+        found[0] += jnp.where(hits[0], place, 0)
+        found[1] += jnp.where(hits[1], place, 0)
+        found[2] += jnp.where(hits[0], pick, 0)
+        found[3] += jnp.where(hits[2], pick, 0)
+        fits = jnp.where(block_l == inside, jnp.where(block_p == p, 1, 0), 0)
+        target += fits * jnp.where(holder == me, near_dest[p:p + 1], 0)
+    lane_of = lax.broadcasted_iota(jnp.int32, (rows, 128), 1)
+    table = jnp.zeros((rows, 128), jnp.int32)
+    for k in range(4):
+        most = count - 1 if k < 2 else secs - 1
+        value = jnp.minimum(jnp.sum(found[k], axis=1, keepdims=True), most)
+        table += jnp.where(lane_of == k, value, 0)
+    lists[0:rows, :] = table
+    owner = lax.div(lax.broadcasted_iota(jnp.int32, (pairs, total_secs), 1), secs)
+    for way in range(2):
+        sign = 1 - 2 * way
+        origin = lax.rem(z - sign * near + 2 * chips, chips) * 2 + core
+        from_there = jnp.where(dest_ref[...] == origin, choice_ref[...], 0)
+        for j in range(2 * FAR - 1):
+            taker = lax.rem(z + sign * (j // 2 + 1) + chips, chips) * 2
+            taker += core if j % 2 == (0 if j < 2 * FAR - 2 else way) else 1 - core
+            wanted = jnp.where(owner == taker, from_there, 0)
+            wanted = jnp.sum(jnp.sum(wanted, axis=0, keepdims=True), axis=1, keepdims=True)
+            wanted = jnp.minimum(wanted, secs - 1)
+            at = rows + way * (2 * FAR - 1) + j
+            lists[at:at + 1, :] = jnp.broadcast_to(wanted, (1, 128))
+    to_scalars = pltpu.make_async_copy(lists, tab_ref, load_sem.at[5])
+    to_scalars.start()
+    goal = jnp.sum(target, axis=1, keepdims=True)
+    slot = lax.rem(z - lax.shift_right_logical(goal, 1) + chips, chips)
+    order = jnp.where(slot < half, 2 * slot - 1, 2 * (chips - slot))
+    order = jnp.where(slot == 0, 0, jnp.where(slot == half, chips - 1, order))
+    code = order * 2 + jnp.where(lax.rem(goal, 2) == core, 0, 1)
+    code_ref[...] = jnp.broadcast_to(code, (count, 128))
+    pl.semaphore_wait(barrier, greetings)
 
     def ring_copy(way, hop, q):
         if way == 0:
@@ -76,8 +165,29 @@
             device_id_type=MESH,
         )
 
-    def last_way(q):
-        return 0 if q < CHUNKS // 2 else 1
+    def far_copy(way, j):
+        step = j // 2 + 1
+        other = j % 2 if j < 2 * FAR - 2 else way
+        slot = near + step if way == 0 else chips - near - step
+        taker = lax.rem(z + (1 - 2 * way) * step + chips, chips) * 2
+        return pltpu.make_async_remote_copy(
+            src_ref=far.at[way, j],
+            dst_ref=blk.at[other * chips + slot],
+            send_sem=far_send.at[way, j],
+            recv_sem=pair_recv.at[slot] if other else far_recv.at[slot],
+            device_id={"sec": taker + (1 - core if other else core)},
+            device_id_type=MESH,
+        )
+
+    def far_arrived(slot):
+        pltpu.make_async_remote_copy(
+            src_ref=far.at[0, 0],
+            dst_ref=blk.at[slot],
+            send_sem=far_send.at[0, 0],
+            recv_sem=far_recv.at[slot],
+            device_id={"sec": mate},
+            device_id_type=MESH,
+        ).wait_recv()
 
     for q in range(CHUNKS):
         ring_copy(0, 1, q).start()
@@ -93,14 +203,25 @@
             device_id_type=MESH,
         )
 
-    def choose(slot):
+    def shelve(slot):
         for s in range(secs):
             shelf[s] = ring[slot, s]
-        pass_on[slot] = shelf[tab_ref[2, chips + slot]]
+
+    def choose(slot, n):
+        pass_on[slot] = shelf[tab_ref[4 * n, 3]]
         pair_copy(slot).start()
-        blk[slot] = shelf[tab_ref[2, slot]]
-
-    choose(0)
+        blk[slot] = shelf[tab_ref[4 * n, 2]]
+
+    def choose_far(way):
+        takers = 2 * FAR - 1
+        for j in reversed(range(takers)):
+            far[way, j] = shelf[tab_ref[rows + way * takers + j, 0]]
+            far_copy(way, j).start()
+
+    to_scalars.wait()
+
+    shelve(0)
+    choose(0, 0)
 
     low = lax.broadcasted_iota(jnp.int32, (pairs, 128), 1) < 64
 
@@ -110,10 +231,11 @@
         for t in range(cells // 128):
             x = psi_ref[v, l, :, t * 128:(t + 1) * 128].astype(F32)
             r = pltpu.roll(x, 64, 1)
-            wide[v, l, pl.ds(2 * t, pairs, stride=64), :] = jnp.where(low, x, r)
-            wide[v, l, pl.ds(2 * t + 1, pairs, stride=64), :] = jnp.where(low, r, x)
-        return carry
-
+            wide[v, pl.ds(l * (pairs * 64) + 2 * t, pairs, stride=64), :] = jnp.where(low, x, r)
+            wide[v, pl.ds(l * (pairs * 64) + 2 * t + 1, pairs, stride=64), :] = jnp.where(low, r, x)
+        return carry
+
+    loads[3].wait()
     lax.fori_loop(0, vectors * secs, widen, 0)
 
     def pack_left(l, carry):
@@ -123,21 +245,22 @@
             )
         return carry
 
+    loads[4].wait()
     lax.fori_loop(0, secs, pack_left, 0)
     acc[...] = jnp.zeros_like(acc)
     low64 = lax.broadcasted_iota(jnp.int32, (64, 128), 1) < 64
 
-    def rows_of(v, l, p):
-        return wide[v, l, pl.ds(p * 64, 64), :]
+    def rows_of(v, place):
+        return wide[v, pl.ds(place * 64, 64), :]
 
     def pair(slot, n):
         found = []
         tiles = []
         for w in range(2):
-            l = tab_ref[0, w * chips + slot]
-            p = tab_ref[1, w * chips + slot]
+            place = tab_ref[4 * n, w]
+            l = lax.div(place, pairs)
             mat = blk[w * chips + slot]
-            ys = [rows_of(v, l, p) for v in range(vectors)]
+            ys = [rows_of(v, place) for v in range(vectors)]
             tiles.append(ys)
             lhs = jnp.concatenate(
                 [jnp.where(low64, y, 0.0).astype(BF16) for y in ys]
@@ -227,61 +350,80 @@
             value += inbox[batch, g].astype(F32)
         total[batch] = value.astype(BF16)
 
+    def first_pair(h):
+        pair_copy(h - 1).wait_recv()
+
+        @pl.when(h - 1 > near)
+        def _():
+            far_arrived(h - 1)
+
+        pair(h - 1, 2 * (h - 1) - 1 + lax.div(half - h, half - 1))
+
+        @pl.when(jnp.logical_and(lax.rem(h, 2) == 1, h >= 3))
+        def _():
+            finish(lax.div(h - 3, 2))
+
+    def second_pair(h):
+        @pl.when(h >= 2)
+        def _():
+            pair_copy(chips - (h - 1)).wait_recv()
+
+            @pl.when(h - 1 > near)
+            def _():
+                far_arrived(chips - (h - 1))
+
+            pair(chips - (h - 1), 2 * (h - 1))
+
+        @pl.when(jnp.logical_and(lax.rem(h, 2) == 1, h >= 5))
+        def _():
+            gather_sum(lax.div(h - 5, 2))
+
     def turn(h, carry):
         def serve(q):
             for way in range(2):
                 ring_copy(way, h, q).wait_recv()
-                if last_way(q) == way:
+
+                @pl.when(h < near)
+                def _():
                     ring_copy(way, h + 1, q).start()
-                else:
-
-                    @pl.when(h < half - 1)
-                    def _():
-                        ring_copy(way, h + 1, q).start()
 
         for q in range(CHUNKS // 2):
             serve(q)
-        pair_copy(h - 1).wait_recv()
-        first = 2 * (h - 1) - 1 + lax.div(half - h, half - 1)
-        pair(h - 1, first)
-
-        @pl.when(jnp.logical_and(lax.rem(h, 2) == 1, h >= 3))
-        def _():
-            finish(lax.div(h - 3, 2))
-
+        first_pair(h)
         for q in range(CHUNKS // 2, CHUNKS):
             serve(q)
-
-        @pl.when(h >= 2)
-        def _():
-            pair_copy(chips - (h - 1)).wait_recv()
-            pair(chips - (h - 1), 2 * (h - 1))
-
-        choose(h)
-        choose(chips - h)
-
-        @pl.when(jnp.logical_and(lax.rem(h, 2) == 1, h >= 5))
-        def _():
-            gather_sum(lax.div(h - 5, 2))
-
-        return carry
-
-    lax.fori_loop(1, half, turn, 0)
-
-    for q in range(CHUNKS):
-        ring_copy(last_way(q), half, q).wait_recv()
-    choose(half)
-    pair_copy(half - 1).wait_recv()
-    pair(half - 1, 2 * half - 3)
-    pair_copy(half + 1).wait_recv()
-    pair(half + 1, 2 * half - 2)
-    pair_copy(half).wait_recv()
-    pair(half, 2 * half - 1)
-    finish(batches - 1)
-
-    dots[...] = jnp.zeros_like(dots)
+        for way in range(2):
+            slot = h if way == 0 else chips - h
+            shelve(slot)
+
+            @pl.when(h == near)
+            def _():
+                choose_far(way)
+
+            choose(slot, 2 * h - 1 + way)
+        second_pair(h)
+        return carry
+
+    lax.fori_loop(1, near + 1, turn, 0)
+
+    def far_turn(h, carry):
+        first_pair(h)
+        second_pair(h)
+        return carry
+
+    lax.fori_loop(near + 1, half, far_turn, 0)
+
+    for slot, n in ((half - 1, 2 * half - 3), (half + 1, 2 * half - 2), (half, 2 * half - 1)):
+        pair_copy(slot).wait_recv()
+        far_arrived(slot)
+        pair(slot, n)
+
+    lane = lax.broadcasted_iota(jnp.int32, (1, 128), 1)
+    row = jnp.zeros((1, 128), F32)
     for i in range(vectors * vectors):
-        dots[i:i + 1, :] = jnp.sum(acc[i], axis=0, keepdims=True)
+        whole = jnp.sum(jnp.sum(acc[i], axis=0, keepdims=True), axis=1, keepdims=True)
+        row += jnp.where(lane == i, whole, 0.0)
+    dots[...] = row
     if groups > 1:
 
         def dot_copy(step):
@@ -300,9 +442,7 @@
 
         lax.fori_loop(1, groups, send_dots, 0)
     dots_op[op] = dots[...]
-
-    if batches > 1:
-        gather_sum(batches - 2)
+    finish(batches - 1)
 
     if groups > 1:
         pltpu.make_async_remote_copy(
@@ -326,7 +466,8 @@
         device_id_type=MESH,
     )
     core_copy.start()
-    gather_sum(batches - 1)
+    if batches > 1:
+        gather_sum(batches - 2)
     core_copy.wait()
     two[...] = one[...] + dots_core[...]
 
@@ -341,21 +482,27 @@
         ).start()
         return carry
 
-    lax.fori_loop(1, chips, send_chip, 0)
+    def send_chips(step, carry):
+        send_chip(half - step, 0)
+        send_chip(half + step, 0)
+        return carry
+
+    send_chip(half, 0)
+    lax.fori_loop(1, half, send_chips, 0)
     dots_chip[z] = two[...]
-
-    code = idx_ref[...]
+    gather_sum(batches - 1)
+
+    code = code_ref[...]
     second = lax.rem(code, 2) == 1
     base = lax.div(code, 2) * 4
     column = lax.broadcasted_iota(jnp.int32, (64, 128), 1)
-    rows = total.shape[0] * 16
     for v in range(vectors):
         table = total[:, v * 16:(v + 1) * 16, :].reshape(rows, 128)
         got = []
         for i in range(4):
-            hot = jnp.where(column[:idx_ref.shape[0], :rows] == base[:, :rows] + i, 1.0, 0.0).astype(BF16)
+            hot = jnp.where(column[:count, :rows] == base[:, :rows] + i, 1.0, 0.0).astype(BF16)
             got.append(jnp.dot(hot, table, preferred_element_type=F32))
-        lanes = column[:idx_ref.shape[0]] < 64
+        lanes = column[:count] < 64
         for i in range(2):
             x = jnp.where(second, pltpu.roll(got[2 * i], 64, 1), got[2 * i])
             y = jnp.where(second, got[2 * i + 1], pltpu.roll(got[2 * i + 1], 64, 1))
@@ -364,23 +511,21 @@
     def drain(h, carry):
         for q in range(CHUNKS):
             for way in range(2):
-                if last_way(q) == way:
-                    ring_copy(way, h, q).wait_send()
-                else:
-
-                    @pl.when(h < half)
-                    def _():
-                        ring_copy(way, h, q).wait_send()
-
-        return carry
-
-    lax.fori_loop(1, half + 1, drain, 0)
+                ring_copy(way, h, q).wait_send()
+        return carry
+
+    lax.fori_loop(1, near + 1, drain, 0)
+
+    for way in range(2):
+        for j in range(2 * FAR - 1):
+            far_copy(way, j).wait_send()
 
     def drain_pairs(slot, carry):
         pair_copy(slot).wait_send()
         return carry
 
-    lax.fori_loop(0, chips, drain_pairs, 0)
+    lax.fori_loop(0, near + 1, drain_pairs, 0)
+    lax.fori_loop(chips - near, chips, drain_pairs, 0)
 
     pltpu.make_async_remote_copy(
         src_ref=dots_chip.at[pl.ds(0, chips - 1)],
@@ -393,11 +538,11 @@
     value = dots_chip[0]
     for g in range(1, chips):
         value += dots_chip[g]
-    three[...] = jnp.sum(value, axis=1, keepdims=True) * scale
+    value = value * scale
     for v in range(vectors):
         for w in range(vectors):
             i = v * vectors + w
-            sub_ref[v:v + 1, w:w + 1] = three[i:i + 1, :]
+            sub_ref[v:v + 1, w:w + 1] = value[:, i:i + 1]
 
 
 def body(psi, left_ops, right_ops, dest_dev, right_sub):
@@ -407,35 +552,7 @@
     groups = lax.axis_size("op")
     chips = devices // 2
     count = secs * pairs
-    me = lax.axis_index("sec")
-    core = me % 2
-    z = me // 2
-    all_dest = dest_dev.reshape(devices, count)
-    all_sub = right_sub.reshape(devices, count)
-    my_dest = lax.dynamic_index_in_dim(all_dest, me, 0, keepdims=False)
-    my_sub = lax.dynamic_index_in_dim(all_sub, me, 0, keepdims=False)
-    mate = z * 2 + 1 - core
-    mate_dest = lax.dynamic_index_in_dim(all_dest, mate, 0, keepdims=False)
-    mate_sub = lax.dynamic_index_in_dim(all_sub, mate, 0, keepdims=False)
-    slots = jnp.arange(chips, dtype=jnp.int32)
-    source = ((z - slots + chips) % chips) * 2
-    same = source + core
-    both = jnp.concatenate([same, source + 1 - core])
-    places = jnp.arange(count, dtype=jnp.int32)
-    hit = both[:, None] == my_dest[None, :]
-    where = jnp.sum(jnp.where(hit, places[None, :], 0), axis=1)
-    mine = jnp.sum(jnp.where(hit[:chips], my_sub[None, :], 0), axis=1)
-    theirs = jnp.sum(
-        jnp.where(same[:, None] == mate_dest[None, :], mate_sub[None, :], 0), axis=1
-    )
-    tab = jnp.stack([where // pairs, where % pairs, jnp.concatenate([mine, theirs])])
-    slot = (z - my_dest // 2 + chips) % chips
     half = chips // 2
-    order = jnp.where(
-        slot == 0, 0, jnp.where(slot == half, chips - 1, jnp.where(slot < half, 2 * slot - 1, 2 * (chips - slot)))
-    )
-    code = order * 2 + (my_dest % 2 != core).astype(jnp.int32)
-    idx = jnp.broadcast_to(code[:, None], (count, 128))
     entries = secs * devices * pairs * cells
     batches = chips // 4
     vmem = pltpu.VMEM
@@ -446,30 +563,40 @@
             jax.ShapeDtypeStruct((vectors, count, cells // 16), BF16),
             jax.ShapeDtypeStruct((vectors, vectors), F32),
         ),
-        in_specs=[pl.BlockSpec(memory_space=pltpu.SMEM)]
-        + [pl.BlockSpec(memory_space=pltpu.VMEM)] * 4,
+        in_specs=[pl.BlockSpec(memory_space=pl.ANY)] * 5,
         out_specs=(pl.BlockSpec(memory_space=pltpu.VMEM), pl.BlockSpec(memory_space=pltpu.VMEM)),
         scratch_shapes=[
+            vmem(psi.shape, BF16),
+            vmem(left_ops.shape, BF16),
+            vmem(right_ops.shape, BF16),
+            vmem((pairs, secs * devices), jnp.int32),
+            vmem((pairs, secs * devices), jnp.int32),
+            vmem((4 * chips + 16, 128), jnp.int32),
+            pltpu.SMEM((4 * chips + 16, 128), jnp.int32),
+            vmem((count, 128), jnp.int32),
             vmem((chips, secs, 128, 128), BF16),
+            vmem((2, 2 * FAR - 1, 128, 128), BF16),
             vmem((2 * chips, 128, 128), BF16),
             vmem((chips, 128, 128), BF16),
-            vmem((vectors, secs, pairs * 64, 128), F32),
+            vmem((vectors, count * 64, 128), F32),
             vmem((secs, 128, 128), BF16),
             vmem((4, vectors, 64, 128), F32),
             vmem((batches, 16, vectors * 16, 128), BF16),
             vmem((batches, groups, vectors * 16, 128), BF16),
             vmem((batches, vectors * 16, 128), BF16),
             vmem((vectors * vectors, 8, 128), F32),
-            vmem((16, 128), F32),
-            vmem((groups, 16, 128), F32),
-            vmem((16, 128), F32),
-            vmem((chips, 16, 128), F32),
-            vmem((16, 128), F32),
-            vmem((16, 128), F32),
-            vmem((16, 1), F32),
+            vmem((1, 128), F32),
+            vmem((groups, 1, 128), F32),
+            vmem((1, 128), F32),
+            vmem((chips, 1, 128), F32),
+            vmem((1, 128), F32),
+            vmem((1, 128), F32),
             vmem((secs, 128, 128), BF16),
+            dma((6,)),
             dma((2, half + 1, CHUNKS)),
             dma((2, half + 1, CHUNKS)),
+            dma((2, 2 * FAR - 1)),
+            dma((chips,)),
             dma((chips,)),
             dma((chips,)),
             dma((batches,)),
@@ -478,12 +605,12 @@
             dma((3,)),
         ],
         compiler_params=pltpu.CompilerParams(
-            collective_id=0, has_side_effects=True, vmem_limit_bytes=48 * 1024 * 1024
+            collective_id=0, has_side_effects=True, vmem_limit_bytes=56 * 1024 * 1024
         ),
         cost_estimate=pl.CostEstimate(
             flops=4 * terms * vectors * count * 64 ** 3, bytes_accessed=8 << 20, transcendentals=0
         ),
-    )(tab, idx, psi, left_ops, right_ops)
+    )(psi, left_ops, right_ops, dest_dev.T, right_sub.T)
     return sigma.reshape(vectors, secs, pairs, cells // 16), subspace
 
 

time: 170 us -> 134 us (0.79)
  Pallas kernels: 162 us -> 130 us
  local copies, waits for them, and re-layouts: 6.74 us -> 2.8 us
    pallas_call x1, Pallas kernels: 162 us -> 130 us  [body(): pl.pallas_call(functools.partial(kernel, chips, groups, 1.0 / entries), o...]
    unnamed x10 -> x2, local copies, waits for them, and re-layouts: 6.39 us -> 2.8 us
where the time goes in v2:
time: 134 us
  Pallas kernels  130 us (97%)
  local copies, waits for them, and re-layouts  2.8 us (2%)
    pallas_call x1, Pallas kernels, body(): pl.pallas_call(functools.partial(kernel, chips, groups, 1.0 / entries), o...  130 us
    unnamed x2, local copies, waits for them, and re-layouts  2.8 us

profile of v2, /device:TPU:1, one launch (start us, length us, event | category | flops | bytes accessed | tf_op | source)
XLA Modules:
  0.0 133.7 jit_solution(14067385013449243021)
XLA Ops:
  0.6 130.3 %shard_map.68 = (bf16[3,64,256]{2,1,0:T(8,128)(2,1)}, f32[3,3]{1,0:T(4,128)}) custom-call(bf16[3,8,8,4096]{3,2,1,0:T(8,128)(2,1)} %psi_hbm.1, bf16[4,8,64,64]{3,2,1,0:T(8,128)(2,1)} %left_hbm.1, bf16[4,8,64,64]{3,2,1,0:T(8,128)(2,1)} %right_hbm.1, s32[8,512]{1,0:T(8,128)} %bitcast.4, s32[8,512]{1,0:T(8,128)} %bitcast.5), custom_call_target="tpu_custom_call" | custom-call | flops 805306368 | bytes 8388608 | tf_op jit(solution)/shard_map/pallas_call | solution.py:560
  130.9 1.5 %copy.9 = bf16[3,8,8,256]{3,2,1,0:T(8,128)(2,1)} copy(bf16[3,8,8,256]{3,2,1,0:T(8,128)(2,1)} %bitcast.3) | data formatting | bytes 196608
  132.5 1.3 copy.10

commit v3 on v2

--- a/solution.py
+++ b/solution.py
@@ -98,6 +98,9 @@
         odd = lax.rem(n, 2)
         half_n = lax.shift_right_logical(n + odd, 1)
         slot = jnp.where(odd == 1, half_n, chips - half_n)
+        m = jnp.maximum(n - 2 * near, 0)
+        half_m = lax.shift_right_logical(m, 1)
+        slot = jnp.where(m > 0, jnp.where(lax.rem(m, 2) == 1, half + half_m, half - half_m), slot)
         return lax.rem(z - slot + 2 * chips, chips) * 2
 
     source = source_of(step_of((rows, width)))
@@ -146,7 +149,11 @@
     goal = jnp.sum(target, axis=1, keepdims=True)
     slot = lax.rem(z - lax.shift_right_logical(goal, 1) + chips, chips)
     order = jnp.where(slot < half, 2 * slot - 1, 2 * (chips - slot))
-    order = jnp.where(slot == 0, 0, jnp.where(slot == half, chips - 1, order))
+    beyond = slot - half
+    order = jnp.where(
+        jnp.abs(beyond) < FAR, 2 * near + jnp.where(beyond < 0, -2 * beyond, 2 * beyond + 1), order
+    )
+    order = jnp.where(slot == 0, 0, order)
     code = order * 2 + jnp.where(lax.rem(goal, 2) == core, 0, 1)
     code_ref[...] = jnp.broadcast_to(code, (count, 128))
     pl.semaphore_wait(barrier, greetings)
@@ -352,11 +359,6 @@
 
     def first_pair(h):
         pair_copy(h - 1).wait_recv()
-
-        @pl.when(h - 1 > near)
-        def _():
-            far_arrived(h - 1)
-
         pair(h - 1, 2 * (h - 1) - 1 + lax.div(half - h, half - 1))
 
         @pl.when(jnp.logical_and(lax.rem(h, 2) == 1, h >= 3))
@@ -367,11 +369,6 @@
         @pl.when(h >= 2)
         def _():
             pair_copy(chips - (h - 1)).wait_recv()
-
-            @pl.when(h - 1 > near)
-            def _():
-                far_arrived(chips - (h - 1))
-
             pair(chips - (h - 1), 2 * (h - 1))
 
         @pl.when(jnp.logical_and(lax.rem(h, 2) == 1, h >= 5))
@@ -406,17 +403,28 @@
 
     lax.fori_loop(1, near + 1, turn, 0)
 
-    def far_turn(h, carry):
+    def pairs_of(h, carry):
         first_pair(h)
         second_pair(h)
         return carry
 
-    lax.fori_loop(near + 1, half, far_turn, 0)
-
-    for slot, n in ((half - 1, 2 * half - 3), (half + 1, 2 * half - 2), (half, 2 * half - 1)):
+    lax.fori_loop(near + 1, near + 2, pairs_of, 0)
+
+    def far_turn(m, carry):
+        half_m = lax.div(m, 2)
+        slot = half + (2 * lax.rem(m, 2) - 1) * half_m
+        n = 2 * near + m
         pair_copy(slot).wait_recv()
         far_arrived(slot)
         pair(slot, n)
+
+        @pl.when(jnp.logical_and(lax.rem(n, 4) == 3, n < chips - 1))
+        def _():
+            finish(lax.div(n, 4))
+
+        return carry
+
+    lax.fori_loop(1, 2 * FAR, far_turn, 0)
 
     lane = lax.broadcasted_iota(jnp.int32, (1, 128), 1)
     row = jnp.zeros((1, 128), F32)
@@ -466,8 +474,8 @@
         device_id_type=MESH,
     )
     core_copy.start()
-    if batches > 1:
-        gather_sum(batches - 2)
+    for batch in range(max(0, (near - 4) // 2 + 1), batches - 1):
+        gather_sum(batch)
     core_copy.wait()
     two[...] = one[...] + dots_core[...]
 

time: 134 us -> 132 us (0.985)
  Pallas kernels: 130 us -> 128 us
    pallas_call x1, Pallas kernels: 130 us -> 128 us  [body(): pl.pallas_call(functools.partial(kernel, chips, groups, 1.0 / entries), o...]
where the time goes in v3:
time: 132 us; the launch traced here: 131 us
  Pallas kernels  128 us (97%)
  local copies, waits for them, and re-layouts  2.8 us (2%)
    pallas_call x1, Pallas kernels, body(): pl.pallas_call(functools.partial(kernel, chips, groups, 1.0 / entries), o...  128 us
    unnamed x2, local copies, waits for them, and re-layouts  2.8 us

profile of v3, /device:TPU:1, one launch (start us, length us, event | category | flops | bytes accessed | tf_op | source)
XLA Modules:
  0.0 131.4 jit_solution(6794367342911912760)
XLA Ops:
  0.6 128.0 %shard_map.68 = (bf16[3,64,256]{2,1,0:T(8,128)(2,1)}, f32[3,3]{1,0:T(4,128)}) custom-call(bf16[3,8,8,4096]{3,2,1,0:T(8,128)(2,1)} %psi_hbm.1, bf16[4,8,64,64]{3,2,1,0:T(8,128)(2,1)} %left_hbm.1, bf16[4,8,64,64]{3,2,1,0:T(8,128)(2,1)} %right_hbm.1, s32[8,512]{1,0:T(8,128)} %bitcast.4, s32[8,512]{1,0:T(8,128)} %bitcast.5), custom_call_target="tpu_custom_call" | custom-call | flops 805306368 | bytes 8388608 | tf_op jit(solution)/shard_map/pallas_call | solution.py:568
  128.6 1.5 %copy.9 = bf16[3,8,8,256]{3,2,1,0:T(8,128)(2,1)} copy(bf16[3,8,8,256]{3,2,1,0:T(8,128)(2,1)} %bitcast.3) | data formatting | bytes 196608
  130.2 1.3 copy.10

commit v4 on v3

--- a/solution.py
+++ b/solution.py
@@ -210,25 +210,25 @@
             device_id_type=MESH,
         )
 
-    def shelve(slot):
+    def shelve(slot, at):
         for s in range(secs):
-            shelf[s] = ring[slot, s]
-
-    def choose(slot, n):
-        pass_on[slot] = shelf[tab_ref[4 * n, 3]]
+            shelf[at, s] = ring[slot, s]
+
+    def choose(slot, n, at):
+        pass_on[slot] = shelf[at, tab_ref[4 * n, 3]]
         pair_copy(slot).start()
-        blk[slot] = shelf[tab_ref[4 * n, 2]]
+        blk[slot] = shelf[at, tab_ref[4 * n, 2]]
 
     def choose_far(way):
         takers = 2 * FAR - 1
         for j in reversed(range(takers)):
-            far[way, j] = shelf[tab_ref[rows + way * takers + j, 0]]
+            far[way, j] = shelf[way, tab_ref[rows + way * takers + j, 0]]
             far_copy(way, j).start()
 
     to_scalars.wait()
 
-    shelve(0)
-    choose(0, 0)
+    shelve(0, 0)
+    choose(0, 0, 0)
 
     low = lax.broadcasted_iota(jnp.int32, (pairs, 128), 1) < 64
 
@@ -391,13 +391,14 @@
             serve(q)
         for way in range(2):
             slot = h if way == 0 else chips - h
-            shelve(slot)
+            shelve(slot, way)
 
             @pl.when(h == near)
             def _():
                 choose_far(way)
 
-            choose(slot, 2 * h - 1 + way)
+        for way in range(2):
+            choose(h if way == 0 else chips - h, 2 * h - 1 + way, way)
         second_pair(h)
         return carry
 
@@ -599,7 +600,7 @@
             vmem((chips, 1, 128), F32),
             vmem((1, 128), F32),
             vmem((1, 128), F32),
-            vmem((secs, 128, 128), BF16),
+            vmem((2, secs, 128, 128), BF16),
             dma((6,)),
             dma((2, half + 1, CHUNKS)),
             dma((2, half + 1, CHUNKS)),

time: 132 us -> 132 us (level)
  no operation moved by 1% of the time
where the time goes in v4:
time: 132 us; the launch traced here: 131 us
  Pallas kernels  128 us (97%)
  local copies, waits for them, and re-layouts  2.8 us (2%)
    pallas_call x1, Pallas kernels, body(): pl.pallas_call(functools.partial(kernel, chips, groups, 1.0 / entries), o...  128 us
    unnamed x2, local copies, waits for them, and re-layouts  2.8 us

profile of v4, /device:TPU:1, one launch (start us, length us, event | category | flops | bytes accessed | tf_op | source)
XLA Modules:
  0.0 131.4 jit_solution(8108681882102711570)
XLA Ops:
  0.6 128.0 %shard_map.68 = (bf16[3,64,256]{2,1,0:T(8,128)(2,1)}, f32[3,3]{1,0:T(4,128)}) custom-call(bf16[3,8,8,4096]{3,2,1,0:T(8,128)(2,1)} %psi_hbm.1, bf16[4,8,64,64]{3,2,1,0:T(8,128)(2,1)} %left_hbm.1, bf16[4,8,64,64]{3,2,1,0:T(8,128)(2,1)} %right_hbm.1, s32[8,512]{1,0:T(8,128)} %bitcast.4, s32[8,512]{1,0:T(8,128)} %bitcast.5), custom_call_target="tpu_custom_call" | custom-call | flops 805306368 | bytes 8388608 | tf_op jit(solution)/shard_map/pallas_call | solution.py:569
  128.6 1.5 %copy.9 = bf16[3,8,8,256]{3,2,1,0:T(8,128)(2,1)} copy(bf16[3,8,8,256]{3,2,1,0:T(8,128)(2,1)} %bitcast.3) | data formatting | bytes 196608
  130.1 1.3 copy.10
